TPU v7x, 32 devices: a whole 2x2x4 slice. The times are simulated.
32 devices in a mesh: req: 4 (over y, x), mdl: 8 (over z, core).
Axes of the slice: x: 2, y: 2, z: 4, core: 2. Of those that a mesh axis runs over, the one named last changes fastest.
Arguments:
- tokens: bfloat16 [8192, 1536], P(('req', 'mdl')), may hold values from -3 to 3
- attention_gain: bfloat16 [1536], replicated, may hold values from 0.099609375 to 1.8984375
- feed_gain: bfloat16 [1536], replicated, may hold values from 0.099609375 to 1.8984375
- w_query: bfloat16 [1536, 1536], P('req', 'mdl'), may hold values from -0.4375 to 0.4375
- w_key: bfloat16 [1536, 768], P('req', 'mdl'), may hold values from -0.15625 to 0.15625
- w_value: bfloat16 [1536, 768], P('req', 'mdl'), may hold values from -0.15625 to 0.15625
- w_out: bfloat16 [1536, 1536], P('mdl', 'req'), may hold values from -0.15625 to 0.15625
- w_gate: bfloat16 [1536, 4096], P('req', 'mdl'), may hold values from -0.15625 to 0.15625
- w_up: bfloat16 [1536, 4096], P('req', 'mdl'), may hold values from -0.15625 to 0.15625
- w_down: bfloat16 [4096, 1536], P('mdl', 'req'), may hold values from -0.09375 to 0.09375
- prefix_cache: bfloat16 [2, 4, 4096, 768], P(None, 'req', None, 'mdl'), may hold values from -400 to 400
- lengths: int32 [16], replicated, may hold values from 0 to 512, as said below
- member: int32 [16], replicated, may hold values from 0 to 3
- owners: int32 [4], replicated, may hold values from 0 to 3, as said below
Outputs:
- hidden: bfloat16 [8192, 1536], P(('req', 'mdl'))
- suffix_cache: bfloat16 [2, 8192, 768], P(None, 'req', 'mdl')
Inputs may be any that keep to these rules, and one draw needn't show every extreme that they name: `lengths`: some request has 512 live tokens in every draw. Request r reads the prefix of group member[r]. Each slot holds exactly one group: slot owners[g] of prefix_cache holds group g's prefix, whose keys carry rotary encoding at positions 0 to 4095.
All inputs are finite; a program needn't handle non-finite values.
Results may differ from a plain program's by a relative error of at most 0.025.
Values may be sent and summed in bfloat16 or wider, within the bound.
No kernel may reach another device: no remote copies, remote signals or barrier semaphores. Data moves between devices by JAX's collectives and lax.ppermute only.
A program may use at most 128 MiB of HBM per device.

v0:
```python
import math

import jax
import jax.numpy as jnp
from jax import lax
from jax.sharding import PartitionSpec as P

HD = 96
SUF = 512


rope_base = 100000.0
norm_eps = 1e-05
far_below = -1e30


def from_partner(block, axis, bit):
    count = lax.axis_size(axis)
    route = []
    for low in range(count):
        high = low | 1 << bit
        if high != low and high < count:
            route += [(low, high), (high, low)]
    return lax.ppermute(block, axis, route)


def rms_scale(row_values, norm_gain):
    numbers = row_values.astype(jnp.float32)
    mean_square = jnp.mean(numbers * numbers, axis=-1, keepdims=True)
    return numbers * lax.rsqrt(mean_square + norm_eps) * norm_gain.astype(jnp.float32)


def rotate(numbers, positions):
    half_width = numbers.shape[-1] // 2
    frequency = rope_base ** (
        -(jnp.arange(half_width).astype(jnp.float32) * 2.0 / numbers.shape[-1])
    )
    angles = positions[:, None] * frequency[None, :]
    cosine = jnp.cos(angles)[:, None, :]
    sine_part = jnp.sin(angles)[:, None, :]
    lower_half = numbers[..., :half_width]
    upper_half = numbers[..., half_width:]
    return jnp.concatenate(
        [
            lower_half * cosine - upper_half * sine_part,
            upper_half * cosine + lower_half * sine_part,
        ],
        axis=-1,
    )


def prefix_part(query_block, key_rows, value_rows, score_scale):
    scores = (
        jnp.einsum("hid,jd->hij", query_block, key_rows, preferred_element_type=jnp.float32)
        * score_scale
    )
    row_top = jnp.max(scores, axis=-1)
    weights = jnp.exp(scores - row_top[..., None])
    row_total = jnp.sum(weights, axis=-1)
    summed = jnp.einsum(
        "hij,jd->hid", weights.astype(jnp.bfloat16), value_rows, preferred_element_type=jnp.float32
    )
    return (row_top, row_total, summed)


def local(
    tokens,
    attention_gain,
    feed_gain,
    w_query,
    w_key,
    w_value,
    w_out,
    w_gate,
    w_up,
    w_down,
    prefix_cache,
    lengths,
    member,
    owners,
):
    w_query, w_key, w_value, w_gate, w_up = (
        lax.all_gather(w_query, "req", axis=0, tiled=True),
        lax.all_gather(w_key, "req", axis=0, tiled=True),
        lax.all_gather(w_value, "req", axis=0, tiled=True),
        lax.all_gather(w_gate, "req", axis=0, tiled=True),
        lax.all_gather(w_up, "req", axis=0, tiled=True),
    )
    w_out, w_down = (
        lax.all_gather(w_out, "req", axis=1, tiled=True),
        lax.all_gather(w_down, "req", axis=1, tiled=True),
    )
    model_devices = lax.axis_size("mdl")
    model_place = lax.axis_index("mdl")
    group_place = lax.axis_index("req")
    local_rows = tokens.shape[0]
    group_rows = local_rows * model_devices
    local_requests = group_rows // SUF
    query_width = w_query.shape[1]
    heads_here = query_width // HD
    pair_width = w_key.shape[1]
    halves = HD // pair_width
    prefix_length = prefix_cache.shape[2]
    score_scale = 1.0 / math.sqrt(HD)
    stacked_weights = jnp.concatenate([w_query, w_key, w_value], axis=1)
    normed = rms_scale(lax.all_gather(tokens, "mdl", axis=0, tiled=True), attention_gain).astype(
        jnp.bfloat16
    )
    projected = jnp.dot(normed, stacked_weights, preferred_element_type=jnp.float32)
    projected_pair = jnp.stack(
        [
            projected[:, query_width : query_width + pair_width],
            projected[:, query_width + pair_width :],
        ],
        axis=0,
    )
    own_prefix = prefix_cache[:, 0]
    low_half = model_place % 2 == 0
    if halves > 1:
        partner = from_partner(projected_pair.astype(jnp.bfloat16), "mdl", 0).astype(
            projected_pair.dtype
        )
        full_pair = jnp.where(
            low_half,
            jnp.concatenate([projected_pair, partner], axis=2),
            jnp.concatenate([partner, projected_pair], axis=2),
        )
        prefix_partner = from_partner(own_prefix, "mdl", 0)
        prefix_full = jnp.where(
            low_half,
            jnp.concatenate([own_prefix, prefix_partner], axis=2),
            jnp.concatenate([prefix_partner, own_prefix], axis=2),
        )
    else:
        full_pair = projected_pair
        prefix_full = own_prefix
    offsets = jnp.arange(group_rows, dtype=jnp.int32) % SUF
    positions = (offsets + prefix_length).astype(jnp.float32)
    queries = rotate(
        projected[:, :query_width].reshape(group_rows, heads_here, HD), positions
    ).astype(jnp.bfloat16)
    keys_rotated = rotate(full_pair[0].reshape(group_rows, 1, HD), positions).reshape(
        group_rows, HD
    )
    key_rows = keys_rotated.astype(jnp.bfloat16)
    value_rows = full_pair[1].astype(jnp.bfloat16)
    local_lengths = lax.dynamic_slice_in_dim(lengths, group_place * local_requests, local_requests)
    valid = jnp.arange(SUF, dtype=jnp.int32)[None, :] < local_lengths[:, None]
    valid_rows = valid.reshape(group_rows)
    own_start = model_place % halves * pair_width
    key_own = lax.dynamic_slice_in_dim(keys_rotated, own_start, pair_width, 1)
    cache_rows = jnp.stack([key_own, projected_pair[1]], axis=0) * valid_rows[None, :, None].astype(
        jnp.float32
    )
    suffix_cache = cache_rows.astype(jnp.bfloat16)
    query_blocks = queries.reshape(local_requests, SUF, heads_here, HD).transpose(0, 2, 1, 3)
    group_numbers = jnp.arange(owners.shape[0], dtype=jnp.int32)
    every_prefix = lax.all_gather(prefix_full[:, None], "req", axis=1, tiled=True)
    local_members = lax.dynamic_slice_in_dim(member, group_place * local_requests, local_requests)
    slot_ids = jnp.sum(
        jnp.where(local_members[:, None] == group_numbers[None, :], owners[None, :], 0), axis=1
    )

    def attend(request):
        slot_index = slot_ids[request]
        prefix_keys = lax.dynamic_index_in_dim(every_prefix[0], slot_index, 0, keepdims=False)
        prefix_values = lax.dynamic_index_in_dim(every_prefix[1], slot_index, 0, keepdims=False)
        return prefix_part(query_blocks[request], prefix_keys, prefix_values, score_scale)

    prefix_top, prefix_total, prefix_sum = lax.map(
        attend, jnp.arange(local_requests, dtype=jnp.int32)
    )
    key_blocks = key_rows.reshape(local_requests, SUF, HD)
    value_blocks = value_rows.reshape(local_requests, SUF, HD)
    scores = (
        jnp.einsum("rhid,rjd->rhij", query_blocks, key_blocks, preferred_element_type=jnp.float32)
        * score_scale
    )
    causal = jnp.arange(SUF)[:, None] >= jnp.arange(SUF)[None, :]
    allowed = (causal[None, :, :] & valid[:, None, :])[:, None]
    masked = jnp.where(allowed, scores, far_below)
    row_top = jnp.maximum(prefix_top, jnp.max(masked, axis=-1))
    carried_share = jnp.exp(prefix_top - row_top)
    weights = jnp.where(allowed, jnp.exp(masked - row_top[..., None]), 0.0)
    row_total = carried_share * prefix_total + jnp.sum(weights, axis=-1)
    summed = carried_share[..., None] * prefix_sum + jnp.einsum(
        "rhij,rjd->rhid",
        weights.astype(jnp.bfloat16),
        value_blocks,
        preferred_element_type=jnp.float32,
    )
    head_output = (summed / row_total[..., None]).astype(jnp.bfloat16)
    attended = head_output.transpose(0, 2, 1, 3).reshape(group_rows, query_width)
    attention_own = lax.psum_scatter(
        jnp.dot(attended, w_out, preferred_element_type=jnp.float32).astype(jnp.bfloat16),
        "mdl",
        scatter_dimension=0,
        tiled=True,
    ).astype(jnp.float32)
    residual = (tokens.astype(jnp.float32) + attention_own).astype(jnp.bfloat16)
    normed_mid = rms_scale(lax.all_gather(residual, "mdl", axis=0, tiled=True), feed_gain).astype(
        jnp.bfloat16
    )
    gate_value = jnp.dot(normed_mid, w_gate, preferred_element_type=jnp.float32)
    up_value = jnp.dot(normed_mid, w_up, preferred_element_type=jnp.float32)
    activation = (jax.nn.silu(gate_value) * up_value).astype(jnp.bfloat16)
    feed_own = lax.psum_scatter(
        jnp.dot(activation, w_down, preferred_element_type=jnp.float32).astype(jnp.bfloat16),
        "mdl",
        scatter_dimension=0,
        tiled=True,
    ).astype(jnp.float32)
    own_valid = lax.dynamic_slice_in_dim(valid_rows, model_place * local_rows, local_rows, 0)
    hidden = (
        (residual.astype(jnp.float32) + feed_own) * own_valid[:, None].astype(jnp.float32)
    ).astype(jnp.bfloat16)
    return (hidden, suffix_cache)


def solution(mesh):
    placed = (
        P(("req", "mdl"), None),
        P(),
        P(),
        P("req", "mdl"),
        P("req", "mdl"),
        P("req", "mdl"),
        P("mdl", "req"),
        P("req", "mdl"),
        P("req", "mdl"),
        P("mdl", "req"),
        P(None, "req", None, "mdl"),
        P(),
        P(),
        P(),
    )
    return jax.shard_map(
        local,
        mesh=mesh,
        in_specs=placed,
        out_specs=(P(("req", "mdl"), None), P(None, "req", "mdl")),
        check_vma=False,
    )
```

profile of v0, /device:TPU:0, one launch (start us, length us, event | category | flops | bytes accessed | tf_op | source)
XLA Modules:
  0.0 602.3 jit_solution(15277913659237689511)
XLA Ops:
  10.9 11.3 %all_gather.32 = bf16[1536,96]{0,1:T(8,128)(2,1)S(1)} all-gather(bf16[384,96]{0,1:T(8,128)(2,1)} %param.20), channel_id=1, replica_groups=mesh['req'=4,'mdl'=8] {'req'}, dimensions={0}, use_global_device_ids=true | all-gather | bytes 368640 | tf_op jit(solution)/shard_map/all_gather | solution.py:84
  22.2 9.3 %all_gather.33 = bf16[1536,96]{0,1:T(8,128)(2,1)S(1)} all-gather(bf16[384,96]{0,1:T(8,128)(2,1)} %param.21), channel_id=1, replica_groups=mesh['req'=4,'mdl'=8] {'req'}, dimensions={0}, use_global_device_ids=true | all-gather | bytes 368640 | tf_op jit(solution)/shard_map/all_gather | solution.py:85
  31.5 10.9 %all_gather.31 = bf16[1536,192]{0,1:T(8,128)(2,1)S(1)} all-gather(bf16[384,192]{0,1:T(8,128)(2,1)} %param.19), channel_id=1, replica_groups=mesh['req'=4,'mdl'=8] {'req'}, dimensions={0}, use_global_device_ids=true | all-gather | bytes 737280 | tf_op jit(solution)/shard_map/all_gather | solution.py:83
  42.3 12.0 %all_gather.35 = bf16[192,1536]{1,0:T(8,128)(2,1)} all-gather(bf16[192,384]{1,0:T(8,128)(2,1)} %param.22), channel_id=1, replica_groups=mesh['req'=4,'mdl'=8] {'req'}, dimensions={1}, use_global_device_ids=true | all-gather | bytes 737280 | tf_op jit(solution)/shard_map/all_gather | solution.py:90
  58.0 19.1 %all-gather.7.cloned.1.call-done = bf16[2048,1536]{1,0:T(8,128)(2,1)} async-done(((bf16[256,1536]{1,0:T(8,128)(2,1)}), bf16[2048,1536]{1,0:T(8,128)(2,1)}) %all-gather.7.cloned.1.call-update) | async-done | bytes 6291472 | tf_op jit(solution)/shard_map/all_gather | solution.py:106
  97.4 50.4 %all-gather.9.cloned.1.call-done = bf16[2,4,4096,96]{2,3,1,0:T(8,128)(2,1)} async-done(((bf16[2,1,4096,96]{2,3,1,0:T(8,128)(2,1)}), bf16[2,4,4096,96]{2,3,1,0:T(8,128)(2,1)}) %all-gather.9.cloned.1.call-update) | async-done | bytes 6291472 | tf_op jit(solution)/shard_map/all_gather | solution.py:158
  147.8 116.0 %while.14 = (s32[]{:T(128)}, f32[4,2,512]{2,1,0:T(2,128)S(1)}, f32[4,2,512]{2,1,0:T(2,128)S(1)}, f32[4,2,512,96]{2,3,1,0:T(8,128)}, s32[4]{0:T(128)S(1)}, /*inde...) while((s32[]{:T(128)}, f32[4,2,512]{2,1,0:T(2,128)S(1)}, ...), condition=%wide.region_5.6_spmd, body=%wide.region_2.5_spmd.sunk | while | flops 1644165120 | bytes 132219144 | solution.py:170
  158.5 5.7 copy-done
  168.2 8.6 %fusion.88 = f32[2,512]{1,0:T(2,128)S(1)} fusion(f32[2,512,4096]{2,1,0:T(8,128)} %copy-done, f32[2,512]{1,0:T(2,128)S(1)} %get-tuple-element.146), kind=kLoop, calls=%fused_computation.3.clone.1 | loop fusion | flops 12581888 | bytes 16785408 | tf_op jit(solution)/shard_map/while/body/eval_jaxpr/reduce_sum | solution.py:59
  187.5 5.7 copy-done
  197.2 8.6 %fusion.88 = f32[2,512]{1,0:T(2,128)S(1)} fusion(f32[2,512,4096]{2,1,0:T(8,128)} %copy-done, f32[2,512]{1,0:T(2,128)S(1)} %get-tuple-element.146), kind=kLoop, calls=%fused_computation.3.clone.1 | loop fusion | flops 12581888 | bytes 16785408 | tf_op jit(solution)/shard_map/while/body/eval_jaxpr/reduce_sum | solution.py:59
  216.5 5.7 copy-done
  226.2 8.6 %fusion.88 = f32[2,512]{1,0:T(2,128)S(1)} fusion(f32[2,512,4096]{2,1,0:T(8,128)} %copy-done, f32[2,512]{1,0:T(2,128)S(1)} %get-tuple-element.146), kind=kLoop, calls=%fused_computation.3.clone.1 | loop fusion | flops 12581888 | bytes 16785408 | tf_op jit(solution)/shard_map/while/body/eval_jaxpr/reduce_sum | solution.py:59
  245.5 5.7 copy-done
  255.2 8.6 %fusion.88 = f32[2,512]{1,0:T(2,128)S(1)} fusion(f32[2,512,4096]{2,1,0:T(8,128)} %copy-done, f32[2,512]{1,0:T(2,128)S(1)} %get-tuple-element.146), kind=kLoop, calls=%fused_computation.3.clone.1 | loop fusion | flops 12581888 | bytes 16785408 | tf_op jit(solution)/shard_map/while/body/eval_jaxpr/reduce_sum | solution.py:59
  274.2 4.5 convolution_convert_fusion
  278.8 69.9 %reduce-scatter.3.cloned.1.call-done = bf16[256,1536]{1,0:T(8,128)(2,1)} async-done(((bf16[2048,1536]{1,0:T(8,128)(2,1)}), bf16[256,1536]{1,0:T(8,128)(2,1)}) %reduce-scatter.3.cloned.1.call-update) | async-done | bytes 786448 | tf_op jit(solution)/shard_map/reduce_scatter | solution.py:194
  352.9 61.3 %all-gather.11.cloned.1.call-done = bf16[2048,1536]{1,0:T(8,128)(2,1)} async-done(((bf16[256,1536]{1,0:T(8,128)(2,1)}), bf16[2048,1536]{1,0:T(8,128)(2,1)}) %all-gather.11.cloned.1.call-update) | async-done | bytes 6291472 | tf_op jit(solution)/shard_map/all_gather | solution.py:201
  418.3 27.3 %all-gather.13.cloned.1.call-done = bf16[1536,512]{1,0:T(8,128)(2,1)} async-done(((bf16[384,512]{1,0:T(8,128)(2,1)}), bf16[1536,512]{1,0:T(8,128)(2,1)}) %all-gather.13.cloned.1.call-update) | async-done | bytes 1572880 | tf_op jit(solution)/shard_map/all_gather | solution.py:86
  445.5 8.7 %fusion.37 = f32[2048,512]{1,0:T(8,128)} fusion(bf16[1536,512]{1,0:T(8,128)(2,1)} %all-gather.13.cloned.1.call-done, bf16[2048,1536]{1,0:T(8,128)(2,1)} %all-gather.11.cloned.1.call-done, f32[1536]{0:T(1024)S(1)} %convert_element_type.140, f32[2048]{0:T(1024)S(1)} %add_rsqrt_fusion), kind=kOutput, calls=%fused_computation.43 | convolution fusion | flops 3233808384 | bytes 12072960 | tf_op jit(solution)/shard_map/dot_general | solution.py:204
  454.2 24.0 %all-gather.15.cloned.1.call-done = bf16[1536,512]{1,0:T(8,128)(2,1)} async-done(((bf16[384,512]{1,0:T(8,128)(2,1)}), bf16[1536,512]{1,0:T(8,128)(2,1)}) %all-gather.15.cloned.1.call-update) | async-done | bytes 1572880 | tf_op jit(solution)/shard_map/all_gather | solution.py:87
  478.2 32.7 %all-gather.17.cloned.1.call-done = bf16[512,1536]{1,0:T(8,128)(2,1)} async-done(((bf16[512,384]{1,0:T(8,128)(2,1)}), bf16[512,1536]{1,0:T(8,128)(2,1)}) %all-gather.17.cloned.1.call-update) | async-done | bytes 1572880 | tf_op jit(solution)/shard_map/all_gather | solution.py:91
  510.9 12.3 %convolution_convert_fusion.1 = bf16[2048,1536]{1,0:T(8,128)(2,1)} fusion(bf16[512,1536]{1,0:T(8,128)(2,1)} %all-gather.17.cloned.1.call-done, f32[2048,512]{1,0:T(8,128)} %fusion.37, bf16[1536,512]{1,0:T(8,128)(2,1)} %all-gather.15.cloned.1.call-done, bf16[2048,1536]{1,0:T(8,128)(2,1)} %all-gather.11.cloned.1.call-done, ...), kind=kOutput, calls=%fused_computation.32 | convolution fusion | flops 6464471040 | bytes 19937280 | tf_op jit(solution)/shard_map/dot_general | solution.py:208
  525.6 67.6 %reduce-scatter.5.cloned.1.call-done = bf16[256,1536]{1,0:T(8,128)(2,1)} async-done(((bf16[2048,1536]{1,0:T(8,128)(2,1)}), bf16[256,1536]{1,0:T(8,128)(2,1)}) %reduce-scatter.5.cloned.1.call-update) | async-done | bytes 786448 | tf_op jit(solution)/shard_map/reduce_scatter | solution.py:207
  (116 shorter events, 94.2 us)
Async XLA Ops:
  7.2 70.0 %all-gather.7.cloned.1.call-start = ((), (), s32[]{:S(2)}) async-start(), calls=%async_computation.2 | async-start | bytes 7077888 | tf_op jit(solution)/shard_map/all_gather | solution.py:106
  7.9 139.9 %all-gather.9.cloned.1.call-start = ((), (), s32[]{:S(2)}) async-start(), calls=%async_computation.3 | async-start | bytes 7864320 | tf_op jit(solution)/shard_map/all_gather | solution.py:158
  8.6 340.0 %reduce-scatter.3.cloned.1.call-start = ((), (), s32[]{:S(2)}) async-start(), calls=%async_computation.4 | async-start | bytes 7077888 | tf_op jit(solution)/shard_map/reduce_scatter | solution.py:194
  77.1 4.6 copy-start.2
  84.6 1.8 copy-start.3
  92.5 0.8 copy-start.4
  92.5 1.0 copy-start.6
  158.5 5.7 copy-start
  187.5 5.7 copy-start
  216.5 5.7 copy-start
  245.5 5.7 copy-start
  266.5 2.3 copy-start.12
  268.8 5.3 copy-start.10
  274.1 74.5 %copy-start.8 = (bf16[256,1536]{1,0:T(8,128)(2,1)S(1)}, bf16[256,1536]{1,0:T(8,128)(2,1)}, u32[]{:S(2)}) copy-start(bf16[256,1536]{1,0:T(8,128)(2,1)} %param.16) | copy-start | bytes 2359300
  278.7 74.2 %copy-start.14 = (bf16[1536]{0:T(1024)(128)(2,1)S(1)}, bf16[1536]{0:T(1024)(128)(2,1)}, u32[]{:S(2)}) copy-start(bf16[1536]{0:T(1024)(128)(2,1)} %param.18) | copy-start | bytes 9220
  278.7 135.5 %all-gather.11.cloned.1.call-start = ((), (), s32[]{:S(2)}) async-start(), calls=%async_computation.5 | async-start | bytes 7077888 | tf_op jit(solution)/shard_map/all_gather | solution.py:201
  350.9 94.6 %all-gather.13.cloned.1.call-start = ((), (), s32[]{:S(2)}) async-start(), calls=%async_computation.6 | async-start | bytes 1966080 | tf_op jit(solution)/shard_map/all_gather | solution.py:86
  351.5 126.7 %all-gather.15.cloned.1.call-start = ((), (), s32[]{:S(2)}) async-start(), calls=%async_computation.7 | async-start | bytes 1966080 | tf_op jit(solution)/shard_map/all_gather | solution.py:87
  352.1 158.8 %all-gather.17.cloned.1.call-start = ((), (), s32[]{:S(2)}) async-start(), calls=%async_computation.8 | async-start | bytes 1966080 | tf_op jit(solution)/shard_map/all_gather | solution.py:91
  352.8 240.4 %reduce-scatter.5.cloned.1.call-start = ((), (), s32[]{:S(2)}) async-start(), calls=%async_computation.9 | async-start | bytes 7077888 | tf_op jit(solution)/shard_map/reduce_scatter | solution.py:207
  523.2 1.0 copy-start.5
  523.2 1.1 copy-start.7
  523.2 1.4 copy-start.9
  523.2 70.0 %copy-start.1 = (bf16[256,1536]{1,0:T(8,128)(2,1)S(1)}, bf16[256,1536]{1,0:T(8,128)(2,1)}, u32[]{:S(2)}) copy-start(bf16[256,1536]{1,0:T(8,128)(2,1)} %add_convert_fusion) | copy-start | bytes 2359300
  (2 other events, 1.4 us)
Sparse Core Ops, SparseCore 0:
  9.6 67.4 all-gather.6
  79.0 68.7 all-gather.8
  278.8 69.7 reduce-scatter.2
  351.0 63.1 all-gather.10
  415.9 29.6 all-gather.12
  447.2 30.9 all-gather.14
  480.0 30.8 all-gather.16
  523.3 69.8 reduce-scatter.4
where the time goes:
time: 603 us; the launch traced here: 602 us
  waiting for transfers between devices  355 us (59%)
  matrix products  61.1 us (10%)
  other arithmetic  57.7 us (10%)
  local copies, waits for them, and re-layouts  54.7 us (9%)
  blocking collectives  43.5 us (7%)
  loops' own time  15.1 us (3%)
  between operations  14.4 us (2%)
    reduce_scatter x1, waiting for transfers between devices, local(): lax.psum_scatter(jnp.dot(attended, w_out, preferred_element_type=jnp.floa...  69.9 us
    reduce_scatter x1, waiting for transfers between devices, local(): lax.psum_scatter(jnp.dot(activation, w_down, preferred_element_type=jnp.f...  67.6 us
    all_gather x1, waiting for transfers between devices, local(): lax.all_gather(residual, 'mdl', axis=0, tiled=True)  61.3 us
    all_gather x1, waiting for transfers between devices, local(): lax.all_gather(prefix_full[:, None], 'req', axis=1, tiled=True)  50.4 us
    reduce_sum x4, other arithmetic, prefix_part(): row_total = jnp.sum(weights, axis=-1)  34.5 us
    all_gather x1, waiting for transfers between devices, local(): lax.all_gather(w_down, 'req', axis=1, tiled=True)  32.7 us
    all_gather x1, waiting for transfers between devices, local(): lax.all_gather(w_gate, 'req', axis=0, tiled=True)  27.3 us
    all_gather x1, waiting for transfers between devices, local(): lax.all_gather(w_up, 'req', axis=0, tiled=True)  24 us
  transfers between devices with their start and end apart: 8, of which 8 were waited for; matrix products, arithmetic and copies ran while one was open for 6% of the time, Pallas kernels for 0%

commit v1 on v0

--- a/solution.py
+++ b/solution.py
@@ -1,8 +1,11 @@
+import functools
 import math
 
 import jax
 import jax.numpy as jnp
 from jax import lax
+from jax.experimental import pallas as pl
+from jax.experimental.pallas import tpu as pltpu
 from jax.sharding import PartitionSpec as P
 
 HD = 96
@@ -217,6 +220,549 @@
     return (hidden, suffix_cache)
 
 
+def any_specs(count):
+    return [pl.BlockSpec(memory_space=pl.ANY)] * count
+
+
+def device_call(kernel, outputs, in_specs, scratch, flops, moved):
+    return pl.pallas_call(
+        kernel,
+        out_shape=outputs,
+        grid_spec=pltpu.PrefetchScalarGridSpec(
+            num_scalar_prefetch=1,
+            grid=(1,),
+            in_specs=in_specs,
+            out_specs=jax.tree.map(
+                lambda out: pl.BlockSpec(out.shape, lambda *_: (0,) * len(out.shape)), outputs
+            ),
+            scratch_shapes=scratch,
+        ),
+        compiler_params=pltpu.CompilerParams(vmem_limit_bytes=48 * 1024 * 1024),
+        cost_estimate=pl.CostEstimate(
+            flops=int(flops), bytes_accessed=int(moved), transcendentals=0
+        ),
+    )
+
+
+def whole_spec(array):
+    return pl.BlockSpec(array.shape, lambda *_: (0,) * array.ndim)
+
+
+def across_first(index, count):
+    return [(place, place ^ index) for place in range(count)]
+
+
+def dot_rows(left, right):
+    return lax.dot_general(left, right, (((1,), (1,)), ((), ())), preferred_element_type=jnp.float32)
+
+
+def square_first(block):
+    return (
+        lax.ppermute(block, "req", across_first(1, 4)),
+        lax.ppermute(block, "req", across_first(2, 4)),
+    )
+
+
+def square_second(beside, above):
+    half = beside.shape[0] // 2
+    return (
+        lax.ppermute(above[:half], "req", across_first(1, 4)),
+        lax.ppermute(beside[half:], "req", across_first(2, 4)),
+    )
+
+
+def project_kernel(lines, offsets, idx, *refs):
+    count = len(offsets)
+    row_refs, weight_refs = refs[:count], refs[count : count + 5]
+    cosine_ref, sine_ref, query_ref, cache_ref, rows, weights, row_sems, weight_sems = refs[
+        count + 5 :
+    ]
+    line, core, square = idx[0], idx[1], idx[2]
+    block = row_refs[0].shape[0]
+    depth = weight_refs[0].shape[1]
+    half_out = weight_refs[3].shape[0]
+    full_out = weight_refs[0].shape[0]
+
+    def weight_copies():
+        copies = []
+        for number, (flip, start, size) in enumerate(
+            [(0, 0, full_out), (1, 0, full_out), (2, 0, full_out), (3, 0, half_out), (3, half_out, half_out)]
+        ):
+            columns = pl.ds(pl.multiple_of((square ^ flip) * depth, 128), depth)
+            copies.append(
+                pltpu.make_async_copy(
+                    weight_refs[number],
+                    weights.at[pl.ds(start, size), columns],
+                    weight_sems.at[number],
+                )
+            )
+        return copies
+
+    def row_copy(number):
+        offset, flip = offsets[number]
+        place = (line + offset) * 2 + (core ^ flip)
+        return pltpu.make_async_copy(
+            row_refs[number],
+            rows.at[pl.ds(pl.multiple_of(place * block, 16), block), :],
+            row_sems.at[number],
+        )
+
+    def present(number):
+        there = line + offsets[number][0]
+        return jnp.logical_and(there >= 0, there < lines)
+
+    for copy in weight_copies():
+        copy.start()
+    for number in range(count):
+        pl.when(present(number))(lambda number=number: row_copy(number).start())
+    for copy in weight_copies():
+        copy.wait()
+    for number in range(count):
+        pl.when(present(number))(lambda number=number: row_copy(number).wait())
+    half = HD // 2
+
+    @pl.loop(0, 2 * lines)
+    def _(step):
+        here = pl.ds(pl.multiple_of(step * block, 128), block)
+        within = lax.rem(step, 2) * block
+        columns = pl.ds(pl.multiple_of(within, 128), block)
+        projected = dot_rows(weights[...], rows[here, :])
+        cosine, sine = cosine_ref[:, columns], sine_ref[:, columns]
+
+        def turned(start):
+            lower, upper = projected[start : start + half], projected[start + half : start + HD]
+            return jnp.concatenate(
+                [lower * cosine - upper * sine, upper * cosine + lower * sine], axis=0
+            )
+
+        for head in range(2):
+            query_ref[head, here, :] = turned(head * HD).T.astype(jnp.bfloat16)
+        live = (
+            within + lax.broadcasted_iota(jnp.int32, (HD, block), 1) < idx[3 + lax.div(step, 2)]
+        )
+        cache_ref[0, :, here] = jnp.where(live, turned(2 * HD), 0.0).astype(jnp.bfloat16)
+        cache_ref[1, :, here] = jnp.where(live, projected[3 * HD :], 0.0).astype(jnp.bfloat16)
+
+
+def attend_kernel(
+    idx,
+    query_all,
+    cache_all,
+    own,
+    beside,
+    above,
+    far_key,
+    far_value,
+    same_ref,
+    other_ref,
+    queries,
+    suffix,
+    key_buf,
+    value_buf,
+    value_rows,
+    sems,
+):
+    request, source, length, core = idx[0], idx[1], idx[2], idx[3]
+    plen = key_buf.shape[1]
+    tail = suffix.shape[2]
+    place = pl.ds(pl.multiple_of(request * tail, 128), tail)
+    copies = [
+        pltpu.make_async_copy(query_all.at[:, place, :], queries, sems.at[0]),
+        pltpu.make_async_copy(cache_all.at[:, :, place], suffix, sems.at[1]),
+    ]
+    for copy in copies:
+        copy.start()
+    keys = [own.at[0], beside.at[0], above.at[0], far_key.at[0]]
+    values = [own.at[1], beside.at[1], above.at[1], far_value.at[0]]
+    for number in range(4):
+
+        @pl.when(source == number)
+        def _(number=number):
+            pltpu.make_async_copy(keys[number], key_buf, sems.at[2]).start()
+            pltpu.make_async_copy(values[number], value_buf, sems.at[3]).start()
+
+    for copy in copies:
+        copy.wait()
+    pltpu.make_async_copy(keys[0], key_buf, sems.at[2]).wait()
+    pltpu.make_async_copy(values[0], value_buf, sems.at[3]).wait()
+
+    def with_ones(piece):
+        lanes = piece.shape[1]
+        marks = (lax.broadcasted_iota(jnp.int32, (128 - HD, lanes), 0) == 0).astype(jnp.float32)
+        return jnp.concatenate([piece.astype(jnp.float32), marks], axis=0).T.astype(jnp.bfloat16)
+
+    step = 512
+
+    @pl.loop(0, plen // step)
+    def _(part):
+        here = pl.ds(pl.multiple_of(part * step, 128), step)
+        value_rows[here, :] = with_ones(value_buf[:, here])
+
+    value_rows[pl.ds(plen, tail), :] = with_ones(suffix[1])
+    factor = math.log2(math.e) / math.sqrt(HD)
+    rows = 128
+    chunk = 1024
+
+    def one_block(start, out_ref, out_start):
+        pair = jnp.concatenate(
+            [queries[0, pl.ds(start, rows), :], queries[1, pl.ds(start, rows), :]], axis=0
+        )
+        top, total = None, None
+        for part in range(plen // chunk + 1):
+            if part < plen // chunk:
+                scores = jnp.dot(
+                    pair,
+                    key_buf[:, part * chunk : (part + 1) * chunk],
+                    preferred_element_type=jnp.float32,
+                )
+                held = value_rows[part * chunk : (part + 1) * chunk, :]
+            else:
+                scores = jnp.dot(pair, suffix[0], preferred_element_type=jnp.float32)
+                row = lax.broadcasted_iota(jnp.int32, scores.shape, 0)
+                row = start + jnp.where(row >= rows, row - rows, row)
+                column = lax.broadcasted_iota(jnp.int32, scores.shape, 1)
+                allowed = jnp.logical_and(column <= row, column < length)
+                scores = jnp.where(allowed, scores, far_below)
+                held = value_rows[plen:, :]
+            highest = jnp.max(scores, axis=1, keepdims=True)
+            new_top = highest if top is None else jnp.maximum(top, highest)
+            weights = jnp.exp2((scores - new_top) * factor).astype(jnp.bfloat16)
+            added = jnp.dot(weights, held, preferred_element_type=jnp.float32)
+            total = (
+                added if total is None else total * jnp.exp2((top - new_top) * factor) + added
+            )
+            top = new_top
+        result = (total[:, :HD] / total[:, HD : HD + 1]).astype(jnp.bfloat16)
+        out_ref[pl.ds(out_start, rows), :] = jnp.concatenate([result[:rows], result[rows:]], axis=1)
+
+    halves = tail // 2
+    for flip, out_ref in enumerate((same_ref, other_ref)):
+
+        @pl.loop(0, halves // rows)
+        def _(part, flip=flip, out_ref=out_ref):
+            out_start = pl.multiple_of(part * rows, rows)
+            start = pl.multiple_of((core ^ flip) * halves + out_start, rows)
+
+            @pl.when(start < length)
+            def _():
+                one_block(start, out_ref, out_start)
+
+            @pl.when(start >= length)
+            def _():
+                out_ref[pl.ds(out_start, rows), :] = jnp.zeros((rows, 2 * HD), jnp.bfloat16)
+
+
+def output_kernel(lines, idx, *refs):
+    pieces = refs[: 2 * lines]
+    weight, tokens, gain, residual_ref, normed_ref = refs[2 * lines :]
+    line, core = idx[0], idx[1]
+    width = pieces[0].shape[1]
+    total = jnp.zeros(tokens.shape, jnp.float32)
+    for number, piece in enumerate(pieces):
+        shift, flip = number // 2, number % 2
+        place = lax.rem(line + lines - shift, lines) * 2 + (core ^ flip)
+        total += jnp.dot(
+            piece[...],
+            weight[pl.ds(pl.multiple_of(place * width, 16), width), :],
+            preferred_element_type=jnp.float32,
+        )
+    residual = (tokens[...].astype(jnp.float32) + total).astype(jnp.bfloat16)
+    residual_ref[...] = residual
+    numbers = residual.astype(jnp.float32)
+    mean_square = jnp.mean(numbers * numbers, axis=-1, keepdims=True)
+    normed_ref[...] = (
+        numbers * lax.rsqrt(mean_square + norm_eps) * gain[...].astype(jnp.float32)
+    ).astype(jnp.bfloat16)
+
+
+def gather_pieces(refs, square, full, split):
+    if len(refs) == 1:
+        return [(refs[0].at[pl.ds(place * full, full), :], place, 0, full) for place in range(4)]
+    return [
+        (refs[0], square, 0, full),
+        (refs[1], square ^ 1, 0, full),
+        (refs[2], square ^ 2, 0, full),
+        (refs[3], square ^ 3, 0, split),
+        (refs[4], square ^ 3, split, full - split),
+    ]
+
+
+def activate_kernel(weight_count, row_count, idx, *refs):
+    weight_refs = refs[:weight_count]
+    row_refs = refs[weight_count : weight_count + row_count]
+    out_ref, gate, up, sems = refs[weight_count + row_count :]
+    square = idx[2]
+    depth = gate.shape[0] // 4
+    copies = []
+    for source, place, first, size in gather_pieces(weight_refs, square, 2 * depth, depth):
+        target = pl.ds(pl.multiple_of(place * depth, 128), depth)
+        if first == 0:
+            copies.append((source.at[pl.ds(0, depth), :], gate.at[target, :]))
+        if first + size == 2 * depth:
+            copies.append((source.at[pl.ds(size - depth, depth), :], up.at[target, :]))
+    copies = [
+        pltpu.make_async_copy(source, target, sems.at[number])
+        for number, (source, target) in enumerate(copies)
+    ]
+    for copy in copies:
+        copy.start()
+    for copy in copies:
+        copy.wait()
+    block = row_refs[0].shape[0]
+    for number, row_ref in enumerate(row_refs):
+        rows = row_ref[...]
+        gated = jnp.dot(rows, gate[...], preferred_element_type=jnp.float32)
+        upper = jnp.dot(rows, up[...], preferred_element_type=jnp.float32)
+        out_ref[number * block : (number + 1) * block, :] = (
+            gated / (1.0 + jnp.exp(-gated)) * upper
+        ).astype(jnp.bfloat16)
+
+
+def down_kernel(counts, block, idx, *refs):
+    first_refs, refs = refs[: counts[0]], refs[counts[0] :]
+    second_refs, refs = refs[: counts[1]], refs[counts[1] :]
+    first_act, second_act, out_a, out_b, first, second, sems = refs
+    square = idx[2]
+    hidden, width = first.shape[0], first.shape[1] // 4
+    copies = []
+    for held, target in ((first_refs, first), (second_refs, second)):
+        for source, place, start, size in gather_pieces(held, square, hidden, hidden // 2):
+            columns = pl.ds(pl.multiple_of(place * width, 128), width)
+            copies.append((source, target.at[pl.ds(start, size), columns]))
+    copies = [
+        pltpu.make_async_copy(source, target, sems.at[number])
+        for number, (source, target) in enumerate(copies)
+    ]
+    for copy in copies:
+        copy.start()
+    for copy in copies:
+        copy.wait()
+    for number, out_ref in enumerate((out_a, out_b)):
+        here = slice(number * block, (number + 1) * block)
+        out_ref[...] = (
+            jnp.dot(first_act[here], first[...], preferred_element_type=jnp.float32)
+            + jnp.dot(second_act[here], second[...], preferred_element_type=jnp.float32)
+        ).astype(jnp.bfloat16)
+
+
+def square_local(
+    tokens,
+    attention_gain,
+    feed_gain,
+    w_query,
+    w_key,
+    w_value,
+    w_out,
+    w_gate,
+    w_up,
+    w_down,
+    prefix_cache,
+    lengths,
+    member,
+    owners,
+):
+    model_devices = lax.axis_size("mdl")
+    lines = model_devices // 2
+    place = lax.axis_index("mdl")
+    square = lax.axis_index("req")
+    line, core = place // 2, place % 2
+    block, width = tokens.shape
+    group_rows = block * model_devices
+    hidden = w_gate.shape[1]
+    plen = prefix_cache.shape[2]
+    bf16 = jnp.bfloat16
+
+    def to_core(array):
+        return lax.ppermute(array, "mdl", across_first(1, model_devices))
+
+    def along(array, step, first=0):
+        route = []
+        for spot in range(lines):
+            began = spot - first if step > 0 else spot + first
+            if 0 <= spot + step < lines and 0 <= began < lines:
+                route += [(2 * spot + side, 2 * (spot + step) + side) for side in range(2)]
+        return lax.ppermute(array, "mdl", route)
+
+    def shifted(array, step, flip):
+        route = []
+        for spot in range(lines):
+            for side in range(2):
+                route.append((2 * spot + side, 2 * ((spot + step) % lines) + (side ^ flip)))
+        return lax.ppermute(array, "mdl", route)
+
+    local_lengths = lax.dynamic_slice_in_dim(lengths, square * lines, lines)
+    local_members = lax.dynamic_slice_in_dim(member, square * lines, lines)
+    group_numbers = jnp.arange(owners.shape[0], dtype=jnp.int32)
+    slot_ids = jnp.sum(
+        jnp.where(local_members[:, None] == group_numbers[None, :], owners[None, :], 0), axis=1
+    )
+    sources = slot_ids ^ square
+    where_am_i = jnp.concatenate([jnp.stack([line, core, square]), local_lengths]).astype(jnp.int32)
+
+    projection = jnp.concatenate([w_query.T, w_key.T, w_value.T], axis=0)
+    projection_beside, projection_above = square_first(projection)
+    prefix = jnp.swapaxes(prefix_cache[:, 0], 1, 2)
+    prefix_beside, prefix_above = square_first(prefix)
+    projection_far = square_second(projection_beside, projection_above)
+
+    normed = rms_scale(tokens, attention_gain).astype(bf16)
+    arrived, offsets = [normed, to_core(normed)], [(0, 0), (0, 1)]
+    upward, downward = normed, normed
+    for step in range(1, lines):
+        upward, downward = along(upward, 1, step - 1), along(downward, -1, step - 1)
+        arrived += [upward, to_core(upward), downward, to_core(downward)]
+        offsets += [(-step, 0), (-step, 1), (step, 0), (step, 1)]
+
+    half = HD // 2
+    frequency = rope_base ** (-(jnp.arange(half).astype(jnp.float32) * 2.0 / HD))
+    positions = (jnp.arange(SUF, dtype=jnp.int32) + plen).astype(jnp.float32)
+    angles = frequency[:, None] * positions[None, :]
+    cosine, sine = jnp.cos(angles), jnp.sin(angles)
+    outputs = (
+        jax.ShapeDtypeStruct((2, group_rows, HD), bf16),
+        jax.ShapeDtypeStruct((2, HD, group_rows), bf16),
+    )
+    queries, cache = device_call(
+        functools.partial(project_kernel, lines, offsets),
+        outputs,
+        any_specs(len(arrived) + 5) + [whole_spec(cosine), whole_spec(sine)],
+        [
+            pltpu.VMEM((group_rows, width), bf16),
+            pltpu.VMEM((4 * HD, width), bf16),
+            pltpu.SemaphoreType.DMA((len(arrived),)),
+            pltpu.SemaphoreType.DMA((5,)),
+        ],
+        2 * group_rows * width * 4 * HD,
+        2 * group_rows * width,
+    )(
+        where_am_i,
+        *arrived,
+        projection,
+        projection_beside,
+        projection_above,
+        *projection_far,
+        cosine,
+        sine,
+    )
+    prefix_far = square_second(prefix_beside, prefix_above)
+
+    gate_up = jnp.concatenate([w_gate, w_up], axis=0)
+    gate_up_z = lax.ppermute(gate_up, "mdl", across_first(4, model_devices))
+    down_z = lax.ppermute(w_down, "mdl", across_first(4, model_devices))
+    late_gate_up, late_down, _ = lax.optimization_barrier((gate_up, w_down, prefix_beside))
+    first_gate_up = [lax.all_gather(late_gate_up, "req", axis=0, tiled=True)]
+    first_down = [lax.all_gather(late_down, "req", axis=0, tiled=True)]
+    gate_up_z, down_z, _ = lax.optimization_barrier((gate_up_z, down_z, prefix_far))
+    gate_up_beside, gate_up_above = square_first(gate_up_z)
+    down_beside, down_above = square_first(down_z)
+    second_gate_up = [
+        gate_up_z,
+        gate_up_beside,
+        gate_up_above,
+        *square_second(gate_up_beside, gate_up_above),
+    ]
+    second_down = [down_z, down_beside, down_above, *square_second(down_beside, down_above)]
+    out_rows = lax.all_gather(w_out, "req", axis=1, tiled=True)
+    out_weight = lax.all_gather(out_rows, "mdl", axis=0, tiled=True)
+
+    pieces = {}
+    for shift in [*range(lines // 2, 0, -1), *range(lines // 2 + 1, lines), 0]:
+        request = (line + shift) % lines
+        facts = jnp.stack(
+            [
+                request,
+                lax.dynamic_index_in_dim(sources, request, 0, False),
+                lax.dynamic_index_in_dim(local_lengths, request, 0, False),
+                core,
+            ]
+        ).astype(jnp.int32)
+        same, other = device_call(
+            attend_kernel,
+            (jax.ShapeDtypeStruct((SUF // 2, 2 * HD), bf16),) * 2,
+            any_specs(7),
+            [
+                pltpu.VMEM((2, SUF, HD), bf16),
+                pltpu.VMEM((2, HD, SUF), bf16),
+                pltpu.VMEM((HD, plen), bf16),
+                pltpu.VMEM((HD, plen), bf16),
+                pltpu.VMEM((plen + SUF, 128), bf16),
+                pltpu.SemaphoreType.DMA((4,)),
+            ],
+            4 * 2 * SUF * plen * 256,
+            4 * plen * HD,
+        )(facts, queries, cache, prefix, prefix_beside, prefix_above, *prefix_far)
+        if shift:
+            pieces[shift] = (shifted(same, shift, 0), shifted(other, shift, 1))
+        else:
+            pieces[shift] = (same, to_core(other))
+    attended = [piece for shift in range(lines) for piece in pieces[shift]]
+    residual, normed_mid = device_call(
+        functools.partial(output_kernel, lines),
+        (jax.ShapeDtypeStruct((block, width), bf16),) * 2,
+        [whole_spec(piece) for piece in attended]
+        + [whole_spec(out_weight), whole_spec(tokens), pl.BlockSpec((1, width), lambda *_: (0, 0))],
+        [],
+        2 * block * width * width,
+        2 * width * width,
+    )(where_am_i, *attended, out_weight, tokens, feed_gain[None, :])
+
+    def to_neighbour(array):
+        return lax.ppermute(array, "mdl", across_first(2, model_devices))
+
+    far_rows = to_neighbour(normed_mid)
+    own_rows = [normed_mid, to_core(normed_mid)]
+    far_rows = [far_rows, to_core(far_rows)]
+
+    def activate(weights, rows):
+        return device_call(
+            functools.partial(activate_kernel, len(weights), len(rows)),
+            jax.ShapeDtypeStruct((len(rows) * block, hidden), bf16),
+            any_specs(len(weights)) + [whole_spec(row) for row in rows],
+            [
+                pltpu.VMEM((width, hidden), bf16),
+                pltpu.VMEM((width, hidden), bf16),
+                pltpu.SemaphoreType.DMA((8,)),
+            ],
+            4 * len(rows) * block * width * hidden,
+            4 * width * hidden,
+        )(where_am_i, *weights, *rows)
+
+    first_own = activate(first_gate_up, own_rows)
+    first_far = activate(first_gate_up, far_rows)
+    second_both = activate(second_gate_up, [*far_rows, *own_rows])
+
+    def down(first_act, part):
+        return device_call(
+            functools.partial(down_kernel, (len(first_down), len(second_down)), block),
+            (jax.ShapeDtypeStruct((block, width), bf16),) * 2,
+            any_specs(len(first_down) + len(second_down))
+            + [
+                whole_spec(first_act),
+                pl.BlockSpec((2 * block, hidden), lambda *_, part=part: (part, 0)),
+            ],
+            [
+                pltpu.VMEM((hidden, width), bf16),
+                pltpu.VMEM((hidden, width), bf16),
+                pltpu.SemaphoreType.DMA((9,)),
+            ],
+            8 * block * width * hidden,
+            4 * width * hidden,
+        )(where_am_i, *first_down, *second_down, first_act, second_both)
+
+    def added(left, right):
+        return left.astype(jnp.float32) + right.astype(jnp.float32)
+
+    far_sum, far_core = down(first_far, 0)
+    far_sum = to_neighbour(added(far_sum, to_core(far_core)).astype(bf16))
+    own_sum, own_core = down(first_own, 1)
+    feed = added(own_sum, to_core(own_core)) + far_sum.astype(jnp.float32)
+    live = core * block + jnp.arange(block, dtype=jnp.int32) < lax.dynamic_index_in_dim(
+        local_lengths, line, 0, False
+    )
+    result = jnp.where(live[:, None], residual.astype(jnp.float32) + feed, 0.0).astype(bf16)
+    return (result, jnp.swapaxes(cache, 1, 2))
+
+
 def solution(mesh):
     placed = (
         P(("req", "mdl"), None),
@@ -234,8 +780,9 @@
         P(),
         P(),
     )
+    square = mesh.shape["req"] == 4 and mesh.shape["mdl"] == 8
     return jax.shard_map(
-        local,
+        square_local if square else local,
         mesh=mesh,
         in_specs=placed,
         out_specs=(P(("req", "mdl"), None), P(None, "req", "mdl")),

time: 603 us -> 361 us (0.60)
  waiting for transfers between devices: 355 us -> 166 us
  Pallas kernels: 0 us -> 86.7 us
  matrix products: 61.1 us -> 0 us
  other arithmetic: 57.7 us -> 12.7 us
  starting transfers between devices: 0.31 us -> 36.8 us
  blocking collectives: 43.5 us -> 15.3 us
  local copies, waits for them, and re-layouts: 54.7 us -> 31.2 us
  loops' own time: 15.1 us -> 0 us
    all_gather x6 -> x3, waiting for transfers between devices: 215 us -> 0.02 us  [the longest x1 0.02 us: square_local(): first_down = [lax.all_gather(late_down, 'req', axis=0, tiled=True)]]
    ppermute x0 -> x44, waiting for transfers between devices: none -> 166 us  [the longest x4 36.9 us: square_first(): lax.ppermute(block, 'req', across_first(1, 4))]
    reduce_scatter x2 -> x0, waiting for transfers between devices: 138 us -> none  [the longest x1 69.9 us: local(): lax.psum_scatter(jnp.dot(attended, w_out, preferred_element_type=jnp.floa...]
    pallas_call x0 -> x11, Pallas kernels: none -> 86.7 us  [the longest x4 49.8 us: square_local(): device_call(attend_kernel, (jax.ShapeDtypeStruct((SUF // 2, 2 * HD), bf16...]
    dot_general x14 -> x0, matrix products: 61.1 us -> none  [the longest x4 15.8 us: prefix_part(): jnp.einsum('hij,jd->hid', weights.astype(jnp.bfloat16), value_rows, prefe...]
    reduce_sum x6 -> x1, other arithmetic: 37.6 us -> 0.18 us  [square_local(): jnp.sum(jnp.where(local_members[:, None] == group_numbers[None, :], owner...]
    ppermute x0 -> x44, starting transfers between devices: none -> 36.7 us  [the longest x6 10.5 us: along(): return lax.ppermute(array, 'mdl', route)]
    all_gather x4 -> x1, blocking collectives: 43.5 us -> 15.3 us  [square_local(): out_rows = lax.all_gather(w_out, 'req', axis=1, tiled=True)]
  transfers between devices with their start and end apart: 8 -> 47, of which waited for: 8 -> 18; matrix products, arithmetic and copies ran while one was open for 6% -> 5% of each run, Pallas kernels for 0% -> 23%
where the time goes in v1:
time: 361 us; the launch traced here: 362 us
  waiting for transfers between devices  166 us (46%)
  Pallas kernels  86.7 us (24%)
  starting transfers between devices  36.8 us (10%)
  local copies, waits for them, and re-layouts  31.2 us (9%)
  blocking collectives  15.3 us (4%)
  between operations  14.2 us (4%)
  other arithmetic  12.7 us (4%)
    pallas_call x4, Pallas kernels, square_local(): device_call(attend_kernel, (jax.ShapeDtypeStruct((SUF // 2, 2 * HD), bf16...  49.8 us
    ppermute x4, waiting for transfers between devices, square_first(): lax.ppermute(block, 'req', across_first(1, 4))  36.9 us
    ppermute x6, waiting for transfers between devices, along(): return lax.ppermute(array, 'mdl', route)  34.5 us
    ppermute x2, waiting for transfers between devices, to_neighbour(): return lax.ppermute(array, 'mdl', across_first(2, model_devices))  33 us
    unnamed x81, local copies, waits for them, and re-layouts  23.1 us
    ppermute x4, waiting for transfers between devices, square_second(): lax.ppermute(beside[half:], 'req', across_first(2, 4))  19.8 us
    all_gather x1, blocking collectives, square_local(): out_rows = lax.all_gather(w_out, 'req', axis=1, tiled=True)  15.3 us
    pallas_call x3, Pallas kernels, activate(): device_call(functools.partial(activate_kernel, len(weights), len(rows)),...  15.1 us
  transfers between devices with their start and end apart: 47, of which 18 were waited for; matrix products, arithmetic and copies ran while one was open for 5% of the time, Pallas kernels for 23%

profile of v1, /device:TPU:0, one launch (start us, length us, event | category | flops | bytes accessed | tf_op | source)
XLA Modules:
  0.0 362.5 jit_solution(6148874094133110776)
XLA Ops:
  7.2 15.3 %all_gather.12 = bf16[192,1536]{1,0:T(8,128)(2,1)} all-gather(bf16[192,384]{1,0:T(8,128)(2,1)} %param.20), channel_id=1, replica_groups=mesh['req'=4,'mdl'=8] {'req'}, dimensions={1}, use_global_device_ids=true | all-gather | bytes 737280 | tf_op jit(solution)/shard_map/all_gather | solution.py:665
  24.7 33.1 %collective-permute-done.17.beside = bf16[2,96,4096]{2,1,0:T(8,128)(2,1)S(1)} collective-permute-done((bf16[2,96,4096]{2,1,0:T(8,128)(2,1)}, bf16[2,96,4096]{2,1,0:T(8,128)(2,1)S(1)}, u32[]{:S(2)}, u32[]{:S(2)}) %collective-permute-start.17) | collective-permute-done | bytes 1572896 | tf_op jit(solution)/shard_map/ppermute | solution.py:261
  67.7 18.0 %collective-permute-done.1.refs_2_ = bf16[256,1536]{1,0:T(8,128)(2,1)S(1)} collective-permute-done((bf16[256,1536]{1,0:T(8,128)(2,1)S(1)}, bf16[256,1536]{1,0:T(8,128)(2,1)S(1)}, u32[]{:S(2)}, u32[]{:S(2)}) %collective-permute-start.1) | collective-permute-done | bytes 786464 | tf_op jit(solution)/shard_map/ppermute | solution.py:584
  91.9 5.2 %collective-permute-done.15.refs_17_ = bf16[192,384]{1,0:T(8,128)(2,1)S(1)} collective-permute-done((bf16[192,384]{1,0:T(8,128)(2,1)S(1)}, bf16[192,384]{1,0:T(8,128)(2,1)S(1)}, u32[]{:S(2)}, u32[]{:S(2)}) %collective-permute-start.15) | collective-permute-done | bytes 147488 | tf_op jit(solution)/shard_map/ppermute | solution.py:269
  97.8 19.0 %collective-permute-done.16.refs_18_ = bf16[192,384]{1,0:T(8,128)(2,1)S(1)} collective-permute-done((bf16[192,384]{1,0:T(8,128)(2,1)S(1)}, bf16[192,384]{1,0:T(8,128)(2,1)S(1)}, u32[]{:S(2)}, u32[]{:S(2)}) %collective-permute-start.16) | collective-permute-done | bytes 147488 | tf_op jit(solution)/shard_map/ppermute | solution.py:270
  124.9 16.2 %collective-permute-done.11.refs_12_ = bf16[256,1536]{1,0:T(8,128)(2,1)} collective-permute-done((bf16[256,1536]{1,0:T(8,128)(2,1)}, bf16[256,1536]{1,0:T(8,128)(2,1)}, u32[]{:S(2)}, u32[]{:S(2)}) %collective-permute-start.11) | collective-permute-done | bytes 786464 | tf_op jit(solution)/shard_map/ppermute | solution.py:584
  162.1 8.7 %shard_map.149 = (bf16[2,2048,96]{2,1,0:T(8,128)(2,1)}, bf16[2,96,2048]{2,1,0:T(8,128)(2,1)}) custom-call(s32[7]{0:T(128)S(1)} %pad_add_fusion.idx, bf16[256,1536]{1,0:T(8,128)(2,1)S(1)} %fusion.2.refs_0_, bf16[256,1536]{1,0:T(8,128)(2,1)S(1)} %copy-done.2, bf16[256,1536]{1,0:T(8,128)(2,1)S(1)} %collective-permute-done.1.refs_2_, ...), custom_call_target="tpu_custom_call" | custom-call | flops 2415919104 | bytes 6291456 | tf_op jit(solution)/shard_map/pallas_call | solution.py:625
  175.2 12.4 %shard_map.153 = (bf16[256,192]{1,0:T(8,128)(2,1)S(1)}, bf16[256,192]{1,0:T(8,128)(2,1)S(1)}) custom-call(s32[4]{0:T(128)S(1)} %get-tuple-element.56.idx, bf16[2,2048,96]{2,1,0:T(8,128)(2,1)S(1)} %copy-done.17, bf16[2,96,2048]{2,1,0:T(8,128)(2,1)S(1)} %copy-done.18, bf16[2,96,4096]{2,1,0:T(8,128)(2,1)} %bitcast.9.own, bf16[2,96,4096]{2,1,0:T(8,128)(2,1)} %copy-done.31, ...), custom_call_target="tpu_custom_call" | custom-call | flops 4294967296 | bytes 1572864 | tf_op jit(solution)/shard_map/pallas_call | solution.py:679
  190.6 12.4 %shard_map.152 = (bf16[256,192]{1,0:T(8,128)(2,1)S(1)}, bf16[256,192]{1,0:T(8,128)(2,1)S(1)}) custom-call(s32[4]{0:T(128)S(1)} %get-tuple-element.55.idx, bf16[2,2048,96]{2,1,0:T(8,128)(2,1)S(1)} %copy-done.17, bf16[2,96,2048]{2,1,0:T(8,128)(2,1)S(1)} %copy-done.18, bf16[2,96,4096]{2,1,0:T(8,128)(2,1)} %bitcast.9.own, bf16[2,96,4096]{2,1,0:T(8,128)(2,1)} %copy-done.31, ...), custom_call_target="tpu_custom_call" | custom-call | flops 4294967296 | bytes 1572864 | tf_op jit(solution)/shard_map/pallas_call | solution.py:679
  205.7 12.4 %shard_map.151 = (bf16[256,192]{1,0:T(8,128)(2,1)S(1)}, bf16[256,192]{1,0:T(8,128)(2,1)S(1)}) custom-call(s32[4]{0:T(128)S(1)} %copy-done.14, bf16[2,2048,96]{2,1,0:T(8,128)(2,1)S(1)} %copy-done.17, bf16[2,96,2048]{2,1,0:T(8,128)(2,1)S(1)} %copy-done.18, bf16[2,96,4096]{2,1,0:T(8,128)(2,1)} %bitcast.9.own, bf16[2,96,4096]{2,1,0:T(8,128)(2,1)} %copy-done.31, ...), custom_call_target="tpu_custom_call" | custom-call | flops 4294967296 | bytes 1572864 | tf_op jit(solution)/shard_map/pallas_call | solution.py:679
  218.1 12.6 %shard_map.150 = (bf16[256,192]{1,0:T(8,128)(2,1)S(1)}, bf16[256,192]{1,0:T(8,128)(2,1)S(1)}) custom-call(s32[4]{0:T(128)S(1)} %get-tuple-element.53.idx, bf16[2,2048,96]{2,1,0:T(8,128)(2,1)S(1)} %copy-done.17, bf16[2,96,2048]{2,1,0:T(8,128)(2,1)S(1)} %copy-done.18, bf16[2,96,4096]{2,1,0:T(8,128)(2,1)} %bitcast.9.own, bf16[2,96,4096]{2,1,0:T(8,128)(2,1)} %copy-done.31, ...), custom_call_target="tpu_custom_call" | custom-call | flops 4294967296 | bytes 1572864 | tf_op jit(solution)/shard_map/pallas_call | solution.py:679
  240.9 4.9 %shard_map.154 = (bf16[256,1536]{1,0:T(8,128)(2,1)S(1)}, bf16[256,1536]{1,0:T(8,128)(2,1)S(1)}) custom-call(s32[7]{0:T(128)S(1)} %pad_add_fusion.idx, bf16[256,192]{1,0:T(8,128)(2,1)S(1)} %get-tuple-element.24.refs_0_, bf16[256,192]{1,0:T(8,128)(2,1)S(1)} %collective-permute-done.21.refs_1_, bf16[256,192]{1,0:T(8,128)(2,1)S(1)} %collective-permute-done.22.refs_2_, ...), custom_call_target="tpu_custom_call" | custom-call | flops 1207959552 | bytes 4718592 | tf_op jit(solution)/shard_map/pallas_call | solution.py:699
  245.9 12.4 %collective-permute-done.29.refs_1_ = bf16[512,384]{1,0:T(8,128)(2,1)} collective-permute-done((bf16[512,384]{1,0:T(8,128)(2,1)}, bf16[512,384]{1,0:T(8,128)(2,1)}, u32[]{:S(2)}, u32[]{:S(2)}) %collective-permute-start.29) | collective-permute-done | bytes 393248 | tf_op jit(solution)/shard_map/ppermute | solution.py:651
  260.3 14.0 %collective-permute-done.39.refs_5_.refs_1_ = bf16[256,1536]{1,0:T(8,128)(2,1)S(1)} collective-permute-done((bf16[256,1536]{1,0:T(8,128)(2,1)S(1)}, bf16[256,1536]{1,0:T(8,128)(2,1)S(1)}, u32[]{:S(2)}, u32[]{:S(2)}) %collective-permute-start.39) | collective-permute-done | bytes 786464 | tf_op jit(solution)/shard_map/ppermute | solution.py:710
  274.4 4.5 %collective-permute-done.36.refs_2_ = bf16[768,512]{1,0:T(8,128)(2,1)S(1)} collective-permute-done((bf16[768,512]{1,0:T(8,128)(2,1)}, bf16[768,512]{1,0:T(8,128)(2,1)S(1)}, u32[]{:S(2)}, u32[]{:S(2)}) %collective-permute-start.36) | collective-permute-done | bytes 786464 | tf_op jit(solution)/shard_map/ppermute | solution.py:262
  281.1 5.3 %collective-permute-done.31.refs_3_ = bf16[512,384]{1,0:T(8,128)(2,1)S(1)} collective-permute-done((bf16[512,384]{1,0:T(8,128)(2,1)}, bf16[512,384]{1,0:T(8,128)(2,1)S(1)}, u32[]{:S(2)}, u32[]{:S(2)}) %collective-permute-start.31) | collective-permute-done | bytes 393248 | tf_op jit(solution)/shard_map/ppermute | solution.py:262
  287.4 3.8 %collective-permute-done.30.refs_2_ = bf16[512,384]{1,0:T(8,128)(2,1)S(1)} collective-permute-done((bf16[512,384]{1,0:T(8,128)(2,1)}, bf16[512,384]{1,0:T(8,128)(2,1)S(1)}, u32[]{:S(2)}, u32[]{:S(2)}) %collective-permute-start.30) | collective-permute-done | bytes 393248 | tf_op jit(solution)/shard_map/ppermute | solution.py:261
  291.9 7.0 %collective-permute-done.37.refs_3_ = bf16[384,512]{1,0:T(8,128)(2,1)S(1)} collective-permute-done((bf16[384,512]{1,0:T(8,128)(2,1)S(1)}, bf16[384,512]{1,0:T(8,128)(2,1)S(1)}, u32[]{:S(2)}, u32[]{:S(2)}) %collective-permute-start.37) | collective-permute-done | bytes 393248 | tf_op jit(solution)/shard_map/ppermute | solution.py:269
  300.4 7.3 %shard_map.156.refs_7_ = bf16[1024,512]{1,0:T(8,128)(2,1)} custom-call(s32[7]{0:T(128)S(1)} %pad_add_fusion.idx, bf16[768,512]{1,0:T(8,128)(2,1)} %collective-permute-done.28.refs_0_, bf16[768,512]{1,0:T(8,128)(2,1)S(1)} %collective-permute-done.35.refs_1_, bf16[768,512]{1,0:T(8,128)(2,1)S(1)} %collective-permute-done.36.refs_2_, ...), custom_call_target="tpu_custom_call" | custom-call | flops 3221225472 | bytes 3145728 | tf_op jit(solution)/shard_map/pallas_call | solution.py:717
  312.7 3.9 %shard_map.158.refs_6_ = bf16[512,512]{1,0:T(8,128)(2,1)S(1)} custom-call(s32[7]{0:T(128)S(1)} %pad_add_fusion.idx, bf16[3072,512]{1,0:T(8,128)(2,1)S(1)} %copy-done.15, bf16[256,1536]{1,0:T(8,128)(2,1)S(1)} %copy-done.22, bf16[256,1536]{1,0:T(8,128)(2,1)S(1)} %copy-done.24), custom_call_target="tpu_custom_call" | custom-call | flops 1610612736 | bytes 3145728 | tf_op jit(solution)/shard_map/pallas_call | solution.py:717
  319.8 4.2 %shard_map.159 = (bf16[256,1536]{1,0:T(8,128)(2,1)S(1)}, bf16[256,1536]{1,0:T(8,128)(2,1)S(1)}) custom-call(s32[7]{0:T(128)S(1)} %pad_add_fusion.idx, bf16[2048,384]{1,0:T(8,128)(2,1)} %all-gather.6.cloned.1.call-done.refs_0_, bf16[512,384]{1,0:T(8,128)(2,1)} %collective-permute-done.29.refs_1_, bf16[512,384]{1,0:T(8,128)(2,1)S(1)} %collective-permute-done.30.refs_2_, ...), custom_call_target="tpu_custom_call" | custom-call | flops 1610612736 | bytes 3145728 | tf_op jit(solution)/shard_map/pallas_call | solution.py:735
  324.2 3.9 %shard_map.155.refs_6_ = bf16[512,512]{1,0:T(8,128)(2,1)S(1)} custom-call(s32[7]{0:T(128)S(1)} %pad_add_fusion.idx, bf16[3072,512]{1,0:T(8,128)(2,1)S(1)} %copy-done.16, bf16[256,1536]{1,0:T(8,128)(2,1)S(1)} %get-tuple-element.36.refs_1_.refs_7_, bf16[256,1536]{1,0:T(8,128)(2,1)S(1)} %copy-done.20), custom_call_target="tpu_custom_call" | custom-call | flops 1610612736 | bytes 3145728 | tf_op jit(solution)/shard_map/pallas_call | solution.py:717
  328.1 4.0 %shard_map.157 = (bf16[256,1536]{1,0:T(8,128)(2,1)S(1)}, bf16[256,1536]{1,0:T(8,128)(2,1)S(1)}) custom-call(s32[7]{0:T(128)S(1)} %pad_add_fusion.idx, bf16[2048,384]{1,0:T(8,128)(2,1)} %all-gather.6.cloned.1.call-done.refs_0_, bf16[512,384]{1,0:T(8,128)(2,1)} %collective-permute-done.29.refs_1_, bf16[512,384]{1,0:T(8,128)(2,1)S(1)} %collective-permute-done.30.refs_2_, ...), custom_call_target="tpu_custom_call" | custom-call | flops 1610612736 | bytes 3145728 | tf_op jit(solution)/shard_map/pallas_call | solution.py:735
  334.5 19.0 %collective-permute-done.43 = bf16[256,1536]{1,0:T(8,128)(2,1)} collective-permute-done((bf16[256,1536]{1,0:T(8,128)(2,1)}, bf16[256,1536]{1,0:T(8,128)(2,1)}, u32[]{:S(2)}, u32[]{:S(2)}) %collective-permute-start.43) | collective-permute-done | bytes 786464 | tf_op jit(solution)/shard_map/ppermute | solution.py:710
  (196 shorter events, 88.7 us)
Async XLA Ops:
  7.2 233.7 %all-gather.4.cloned.1.call-start = ((), (), s32[]{:S(2)}) async-start(), calls=%async_computation | async-start | bytes 5308416 | tf_op jit(solution)/shard_map/all_gather | solution.py:666
  22.5 286.0 %all-gather.8.cloned.1.call-start = ((), (), s32[]{:S(2)}) async-start(), calls=%async_computation.2 | async-start | bytes 3932160 | tf_op jit(solution)/shard_map/all_gather | solution.py:653
  22.6 35.2 %collective-permute-start.17 = (bf16[2,96,4096]{2,1,0:T(8,128)(2,1)}, bf16[2,96,4096]{2,1,0:T(8,128)(2,1)S(1)}, u32[]{:S(2)}, u32[]{:S(2)}) collective-permute-start(bf16[2,96,4096]{2,1,0:T(8,128)(2,1)} %bitcast.9.own), channel_id=1, source_target_pairs={{0,8},{8,0},{16,24},{24,16},{1,9},{9,1},{17,25},{25,17},{2,10},{10... | collective-permute-start | bytes 4718600 | tf_op jit(solution)/shard_map/ppermute | solution.py:261
  57.8 259.6 %all-gather.6.cloned.1.call-start = ((), (), s32[]{:S(2)}) async-start(), calls=%async_computation.1 | async-start | bytes 1966080 | tf_op jit(solution)/shard_map/all_gather | solution.py:654
  59.2 26.5 %collective-permute-start.1 = (bf16[256,1536]{1,0:T(8,128)(2,1)S(1)}, bf16[256,1536]{1,0:T(8,128)(2,1)S(1)}, u32[]{:S(2)}, u32[]{:S(2)}) collective-permute-start(bf16[256,1536]{1,0:T(8,128)(2,1)S(1)} %fusion.2.refs_0_), channel_id=1, source_target_pairs={{0,2},{1,3},{2,4},{3,5},{4,6},{5,7},{8,10},{9,11},{10,12},{11,13},... | collective-permute-start | bytes 2359304 | tf_op jit(solution)/shard_map/ppermute | solution.py:584
  66.4 57.9 %collective-permute-start.18 = (bf16[2,96,4096]{2,1,0:T(8,128)(2,1)}, bf16[2,96,4096]{2,1,0:T(8,128)(2,1)}, u32[]{:S(2)}, u32[]{:S(2)}) collective-permute-start(bf16[2,96,4096]{2,1,0:T(8,128)(2,1)} %bitcast.9.own), channel_id=1, source_target_pairs={{0,16},{8,24},{16,0},{24,8},{1,17},{9,25},{17,1},{25,9},{2,18},{10... | collective-permute-start | bytes 4718600 | tf_op jit(solution)/shard_map/ppermute | solution.py:262
  85.7 31.8 %collective-permute-start.5 = (bf16[256,1536]{1,0:T(8,128)(2,1)S(1)}, bf16[256,1536]{1,0:T(8,128)(2,1)}, u32[]{:S(2)}, u32[]{:S(2)}) collective-permute-start(bf16[256,1536]{1,0:T(8,128)(2,1)S(1)} %collective-permute-done.1.refs_2_), channel_id=1, source_target_pairs={{2,4},{3,5},{4,6},{5,7},{10,12},{11,13},{12,14},{13,15},{18,20},{1... | collective-permute-start | bytes 2359304 | tf_op jit(solution)/shard_map/ppermute | solution.py:584
  87.5 31.5 %collective-permute-start.7 = (bf16[256,1536]{1,0:T(8,128)(2,1)S(1)}, bf16[256,1536]{1,0:T(8,128)(2,1)}, u32[]{:S(2)}, u32[]{:S(2)}) collective-permute-start(bf16[256,1536]{1,0:T(8,128)(2,1)S(1)} %collective-permute-done.3.refs_4_), channel_id=1, source_target_pairs={{2,0},{3,1},{4,2},{5,3},{10,8},{11,9},{12,10},{13,11},{18,16},{19,... | collective-permute-start | bytes 2359304 | tf_op jit(solution)/shard_map/ppermute | solution.py:584
  90.4 26.4 %collective-permute-start.16 = (bf16[192,384]{1,0:T(8,128)(2,1)S(1)}, bf16[192,384]{1,0:T(8,128)(2,1)S(1)}, u32[]{:S(2)}, u32[]{:S(2)}) collective-permute-start(bf16[192,384]{1,0:T(8,128)(2,1)S(1)} %slice.33), channel_id=1, source_target_pairs={{0,16},{8,24},{16,0},{24,8},{1,17},{9,25},{17,1},{25,9},{2,18},{10... | collective-permute-start | bytes 442376 | tf_op jit(solution)/shard_map/ppermute | solution.py:270
  121.2 26.8 %collective-permute-start.4 = (bf16[256,1536]{1,0:T(8,128)(2,1)S(1)}, bf16[256,1536]{1,0:T(8,128)(2,1)}, u32[]{:S(2)}, u32[]{:S(2)}) collective-permute-start(bf16[256,1536]{1,0:T(8,128)(2,1)S(1)} %collective-permute-done.3.refs_4_), channel_id=1, source_target_pairs={{0,1},{1,0},{2,3},{3,2},{4,5},{5,4},{6,7},{7,6},{8,9},{9,8},{10,11... | collective-permute-start | bytes 2359304 | tf_op jit(solution)/shard_map/ppermute | solution.py:576
  122.6 26.0 %collective-permute-start.6 = (bf16[256,1536]{1,0:T(8,128)(2,1)}, bf16[256,1536]{1,0:T(8,128)(2,1)}, u32[]{:S(2)}, u32[]{:S(2)}) collective-permute-start(bf16[256,1536]{1,0:T(8,128)(2,1)} %collective-permute-done.5.refs_6_), channel_id=1, source_target_pairs={{0,1},{1,0},{2,3},{3,2},{4,5},{5,4},{6,7},{7,6},{8,9},{9,8},{10,11... | collective-permute-start | bytes 2359304 | tf_op jit(solution)/shard_map/ppermute | solution.py:576
  124.3 29.4 %collective-permute-start.8 = (bf16[256,1536]{1,0:T(8,128)(2,1)}, bf16[256,1536]{1,0:T(8,128)(2,1)}, u32[]{:S(2)}, u32[]{:S(2)}) collective-permute-start(bf16[256,1536]{1,0:T(8,128)(2,1)} %collective-permute-done.7.refs_8_), channel_id=1, source_target_pairs={{0,1},{1,0},{2,3},{3,2},{4,5},{5,4},{6,7},{7,6},{8,9},{9,8},{10,11... | collective-permute-start | bytes 2359304 | tf_op jit(solution)/shard_map/ppermute | solution.py:576
  124.8 30.3 %collective-permute-start.10 = (bf16[256,1536]{1,0:T(8,128)(2,1)}, bf16[256,1536]{1,0:T(8,128)(2,1)}, u32[]{:S(2)}, u32[]{:S(2)}) collective-permute-start(bf16[256,1536]{1,0:T(8,128)(2,1)} %collective-permute-done.9.refs_10_), channel_id=1, source_target_pairs={{0,1},{1,0},{2,3},{3,2},{4,5},{5,4},{6,7},{7,6},{8,9},{9,8},{10,11... | collective-permute-start | bytes 2359304 | tf_op jit(solution)/shard_map/ppermute | solution.py:576
  153.7 104.6 %collective-permute-start.28 = (bf16[768,512]{1,0:T(8,128)(2,1)}, bf16[768,512]{1,0:T(8,128)(2,1)}, u32[]{:S(2)}, u32[]{:S(2)}) collective-permute-start(bf16[768,512]{1,0:T(8,128)(2,1)} %constant_dynamic-update-slice_fusion), channel_id=1, source_target_pairs={{0,4},{1,5},{2,6},{3,7},{4,0},{5,1},{6,2},{7,3},{8,12},{9,13},{10,... | collective-permute-start | bytes 2359304 | tf_op jit(solution)/shard_map/ppermute | solution.py:650
  187.6 43.1 %collective-permute-start.26 = (bf16[256,192]{1,0:T(8,128)(2,1)S(1)}, bf16[256,192]{1,0:T(8,128)(2,1)S(1)}, u32[]{:S(2)}, u32[]{:S(2)}) collective-permute-start(bf16[256,192]{1,0:T(8,128)(2,1)S(1)} %get-tuple-element.30), channel_id=1, source_target_pairs={{0,6},{1,7},{2,0},{3,1},{4,2},{5,3},{6,4},{7,5},{8,14},{9,15},{10,... | collective-permute-start | bytes 294920 | tf_op jit(solution)/shard_map/ppermute | solution.py:591
  190.6 42.0 %collective-permute-start.27 = (bf16[256,192]{1,0:T(8,128)(2,1)S(1)}, bf16[256,192]{1,0:T(8,128)(2,1)S(1)}, u32[]{:S(2)}, u32[]{:S(2)}) collective-permute-start(bf16[256,192]{1,0:T(8,128)(2,1)S(1)} %get-tuple-element.31), channel_id=1, source_target_pairs={{0,7},{1,6},{2,1},{3,0},{4,3},{5,2},{6,5},{7,4},{8,15},{9,14},{10,... | collective-permute-start | bytes 294920 | tf_op jit(solution)/shard_map/ppermute | solution.py:591
  203.0 29.6 %collective-permute-start.24 = (bf16[256,192]{1,0:T(8,128)(2,1)S(1)}, bf16[256,192]{1,0:T(8,128)(2,1)S(1)}, u32[]{:S(2)}, u32[]{:S(2)}) collective-permute-start(bf16[256,192]{1,0:T(8,128)(2,1)S(1)} %get-tuple-element.28), channel_id=1, source_target_pairs={{0,4},{1,5},{2,6},{3,7},{4,0},{5,1},{6,2},{7,3},{8,12},{9,13},{10,... | collective-permute-start | bytes 294920 | tf_op jit(solution)/shard_map/ppermute | solution.py:591
  203.1 29.7 %collective-permute-start.25 = (bf16[256,192]{1,0:T(8,128)(2,1)S(1)}, bf16[256,192]{1,0:T(8,128)(2,1)S(1)}, u32[]{:S(2)}, u32[]{:S(2)}) collective-permute-start(bf16[256,192]{1,0:T(8,128)(2,1)S(1)} %get-tuple-element.29), channel_id=1, source_target_pairs={{0,5},{1,4},{2,7},{3,6},{4,1},{5,0},{6,3},{7,2},{8,13},{9,12},{10,... | collective-permute-start | bytes 294920 | tf_op jit(solution)/shard_map/ppermute | solution.py:591
  232.8 25.5 %collective-permute-start.29 = (bf16[512,384]{1,0:T(8,128)(2,1)}, bf16[512,384]{1,0:T(8,128)(2,1)}, u32[]{:S(2)}, u32[]{:S(2)}) collective-permute-start(bf16[512,384]{1,0:T(8,128)(2,1)} %param.23), channel_id=1, source_target_pairs={{0,4},{1,5},{2,6},{3,7},{4,0},{5,1},{6,2},{7,3},{8,12},{9,13},{10,... | collective-permute-start | bytes 1179656 | tf_op jit(solution)/shard_map/ppermute | solution.py:651
  245.8 28.6 %collective-permute-start.39 = (bf16[256,1536]{1,0:T(8,128)(2,1)S(1)}, bf16[256,1536]{1,0:T(8,128)(2,1)S(1)}, u32[]{:S(2)}, u32[]{:S(2)}) collective-permute-start(bf16[256,1536]{1,0:T(8,128)(2,1)S(1)} %get-tuple-element.36.refs_1_.refs_7_), channel_id=1, source_target_pairs={{0,2},{1,3},{2,0},{3,1},{4,6},{5,7},{6,4},{7,5},{8,10},{9,11},{10,... | collective-permute-start | bytes 2359304 | tf_op jit(solution)/shard_map/ppermute | solution.py:710
  258.3 28.1 %collective-permute-start.31 = (bf16[512,384]{1,0:T(8,128)(2,1)}, bf16[512,384]{1,0:T(8,128)(2,1)S(1)}, u32[]{:S(2)}, u32[]{:S(2)}) collective-permute-start(bf16[512,384]{1,0:T(8,128)(2,1)} %collective-permute-done.29.refs_1_), channel_id=1, source_target_pairs={{0,16},{8,24},{16,0},{24,8},{1,17},{9,25},{17,1},{25,9},{2,18},{10... | collective-permute-start | bytes 1179656 | tf_op jit(solution)/shard_map/ppermute | solution.py:262
  260.3 39.1 %collective-permute-start.34 = (bf16[256,1536]{1,0:T(8,128)(2,1)S(1)}, bf16[256,1536]{1,0:T(8,128)(2,1)S(1)}, u32[]{:S(2)}, u32[]{:S(2)}) collective-permute-start(bf16[256,1536]{1,0:T(8,128)(2,1)S(1)} %get-tuple-element.36.refs_1_.refs_7_), channel_id=1, source_target_pairs={{0,1},{1,0},{2,3},{3,2},{4,5},{5,4},{6,7},{7,6},{8,9},{9,8},{10,11... | collective-permute-start | bytes 2359304 | tf_op jit(solution)/shard_map/ppermute | solution.py:576
  274.4 25.1 %collective-permute-start.40 = (bf16[256,1536]{1,0:T(8,128)(2,1)S(1)}, bf16[256,1536]{1,0:T(8,128)(2,1)S(1)}, u32[]{:S(2)}, u32[]{:S(2)}) collective-permute-start(bf16[256,1536]{1,0:T(8,128)(2,1)S(1)} %collective-permute-done.39.refs_5_.refs_1_), channel_id=1, source_target_pairs={{0,1},{1,0},{2,3},{3,2},{4,5},{5,4},{6,7},{7,6},{8,9},{9,8},{10,11... | collective-permute-start | bytes 2359304 | tf_op jit(solution)/shard_map/ppermute | solution.py:576
  291.2 26.2 %collective-permute-start.32 = (bf16[256,384]{1,0:T(8,128)(2,1)}, bf16[256,384]{1,0:T(8,128)(2,1)S(1)}, u32[]{:S(2)}, u32[]{:S(2)}) collective-permute-start(bf16[256,384]{1,0:T(8,128)(2,1)} %slice.36), channel_id=1, source_target_pairs={{0,8},{8,0},{16,24},{24,16},{1,9},{9,1},{17,25},{25,17},{2,10},{10... | collective-permute-start | bytes 589832 | tf_op jit(solution)/shard_map/ppermute | solution.py:269
  (63 other events, 863.0 us)
Sparse Core Ops, SparseCore 0:
  22.7 54.1 all-gather.3
  79.3 55.6 all-gather.7
  153.8 34.9 all-gather.5
